TPU v7x, 512 devices: a whole 4x4x16 slice. The times are simulated.
512 devices in a mesh: prow: 16 (over x, y), pcol: 32 (over z, core).
Axes of the slice: x: 4, y: 4, z: 16, core: 2. Of those that a mesh axis runs over, the one named last changes fastest.
Arguments:
- matrix: float32 [4096, 32768], P('prow', 'pcol'), may hold values from -6 to 6
- lpanel: float32 [4096, 256], P(('prow', 'pcol')), may hold values from -0.375 to 0.375
- linv: float32 [256, 256], replicated, as said below
- pivots: int32 [256], replicated, may hold values from 256 to 4095, as said below
- weights: float32 [2, 4096], P(None, 'prow'), may hold values from -0.09375 to 0.09375
Outputs:
- updated: float32 [4096, 32768], P('prow', 'pcol')
- checks: float32 [2, 32768], P(None, 'pcol')
Inputs may be any that keep to these rules, and one draw needn't show every extreme that they name: `pivots`: distinct row indices outside the first 256 rows; 256 and 4095 both occur. `linv`: unit lower triangular.
All inputs are finite; a program needn't handle non-finite values.
Results may differ from a plain program's by a relative error of at most 0.000071.
Values sent between devices are 32-bit elements; how exact they have to be, the bound alone decides.
A program may use at most 64 MiB of HBM per device.

v0:
```python
import jax
import jax.numpy as jnp
from jax import lax
from jax.sharding import PartitionSpec as P


def from_root(block, axis, owner):
    block = jnp.where(lax.axis_index(axis) == owner, block, jnp.zeros_like(block))
    return lax.psum(block, axis)


def shards(matrix, lpanel, linv, pivots, weights):
    rows_here = matrix.shape[0]
    panel_width = linv.shape[0]
    row_block = lax.axis_index("prow")
    local_index = pivots - row_block * rows_here
    owned = (local_index >= 0) & (local_index < rows_here)
    safe_index = jnp.clip(local_index, 0, rows_here - 1)
    picked = jnp.where(owned[:, None], matrix[safe_index], 0.0)
    old_top = from_root(matrix, "prow", 0)
    target = jnp.where(owned, local_index, rows_here)
    swapped = matrix.at[target].set(old_top, mode="drop")
    gathered_rows = lax.psum(picked, "prow")
    solved = jnp.dot(
        linv, gathered_rows, precision=lax.Precision.HIGHEST, preferred_element_type=jnp.float32
    )
    lower = swapped - jnp.dot(
        lax.all_gather(lpanel, "pcol", axis=0, tiled=True),
        solved,
        precision=lax.Precision.HIGHEST,
        preferred_element_type=jnp.float32,
    )
    head_rows = jnp.where(row_block == 0, solved, lower)
    updated = lower.at[:panel_width].set(head_rows)
    partial_checks = jnp.dot(
        weights, updated, precision=lax.Precision.HIGHEST, preferred_element_type=jnp.float32
    )
    checks = lax.psum(partial_checks, "prow")
    return (updated, checks)


def solution(mesh):
    return jax.shard_map(
        shards,
        mesh=mesh,
        in_specs=(P("prow", "pcol"), P(("prow", "pcol"), None), P(), P(), P(None, "prow")),
        out_specs=(P("prow", "pcol"), P(None, "pcol")),
        check_vma=False,
    )
```

profile of v0, /device:TPU:32, one launch (start us, length us, event | category | flops | bytes accessed | tf_op | source)
XLA Modules:
  0.0 195.9 jit_solution(3004593779298745947)
XLA Ops:
  7.2 0.0 copy-start
  7.2 0.0 all-reduce.3.cloned.1.call-start
  7.2 1.3 copy.16
  8.5 0.0 copy-start.2
  8.5 0.7 copy-done.2
  9.2 0.3 copy.8
  9.5 2.0 %gather_fusion = f32[256,1024]{1,0:T(8,128)} fusion(f32[256,1024]{1,0:T(8,128)S(1)} %copy.16, s32[1024]{0:T(1024)S(1)} %pad_clamp_fusion), kind=kCustom, calls=%fused_computation | custom fusion | bytes 2098176 | tf_op jit(solution)/shard_map/gather | solution.py:19
  11.6 1.6 copy.7
  13.1 1.5 broadcast_select_fusion
  14.6 0.0 copy-start.1
  14.6 0.0 all-reduce.3.cloned.1.call-update
  14.6 0.7 copy-done.1
  15.3 34.8 %all_gather.3 = f32[256,256]{1,0:T(8,128)S(1)} all-gather(f32[8,256]{1,0:T(8,128)S(1)} %copy-done.1), channel_id=1, replica_groups=mesh['prow'=16,'pcol'=32] {'pcol'}, dimensions={0}, use_global_device_ids=true | all-gather | bytes 270336 | tf_op jit(solution)/shard_map/all_gather | solution.py:28
  50.1 89.9 %all-reduce.3.cloned.1.call-done = (f32[256,1024]{0,1:T(8,128)}, f32[256,1024]{0,1:T(8,128)}) async-done(((f32[256,1024]{0,1:T(8,128)}, f32[256,1024]{0,1:T(8,128)}), (f32[256,1024]{0,1:T(8,128)}, f32[256,1024]{0,1:T(8,128)})) %all-reduce.3.cloned.1.call-update) | async-done | bytes 2097168 | tf_op jit(solution)/shard_map/psum | solution.py:9
  140.0 1.6 copy.9
  141.6 1.9 scatter_fusion
  143.5 0.3 copy.10
  143.9 0.0 copy-done
  143.9 2.2 %fusion.2 = f32[1024,256]{1,0:T(8,128)S(1)} fusion(f32[256,1024]{0,1:T(8,128)} %get-tuple-element.25, f32[256,256]{1,0:T(8,128)S(1)} %copy-done), kind=kOutput, calls=%fused_computation.12 | convolution fusion | flops 805306368 | bytes 2359296 | tf_op jit(solution)/shard_map/dot_general | solution.py:24
  146.1 1.0 fusion.1
  147.2 0.0 copy-start.3
  147.2 1.3 copy.11
  148.5 0.0 copy-done.3
  148.5 1.0 convolution_bitcast_fusion.1
  149.5 39.6 %psum.23 = f32[2,1024]{1,0:T(2,128)} all-reduce(f32[2,1024]{1,0:T(2,128)S(1)} %convolution_bitcast_fusion.1), channel_id=1, replica_groups=mesh['prow'=16,'pcol'=32] {'prow'}, use_global_device_ids=true, to_apply=%region_3.4 | all-reduce | flops 2048 | bytes 16384 | tf_op jit(solution)/shard_map/psum | solution.py:38
  (3 shorter events, 0.0 us)
Async XLA Ops:
  7.2 136.7 %copy-start = (f32[256,256]{1,0:T(8,128)S(1)}, f32[256,256]{1,0:T(8,128)}, u32[]{:S(2)}) copy-start(f32[256,256]{1,0:T(8,128)} %param.11) | copy-start | bytes 786436
  7.2 132.9 %all-reduce.3.cloned.1.call-start = ((), (), s32[]{:S(2)}) async-start(), calls=%async_computation | async-start | bytes 4194304 | tf_op jit(solution)/shard_map/psum | solution.py:9
  8.5 0.7 copy-start.2
  14.6 0.7 copy-start.1
  147.2 1.3 copy-start.3
Sparse Core Ops, SparseCore 0:
  14.7 125.2 all-reduce.2
where the time goes:
time: 196 us
  waiting for transfers between devices  90 us (46%)
  blocking collectives  74.4 us (38%)
  between operations  14.1 us (7%)
  local copies, waits for them, and re-layouts  11.6 us (6%)
  matrix products  4.24 us (2%)
    psum x1, waiting for transfers between devices, from_root(): return lax.psum(block, axis)  89.9 us
    psum x1, blocking collectives, shards(): checks = lax.psum(partial_checks, 'prow')  39.6 us
    all_gather x1, blocking collectives, shards(): lax.all_gather(lpanel, 'pcol', axis=0, tiled=True)  34.8 us
    unnamed x11, local copies, waits for them, and re-layouts  4.26 us
  transfers between devices with their start and end apart: 1, of which 1 were waited for; matrix products, arithmetic and copies ran while one was open for 0% of the time, Pallas kernels for 0%

commit v1 on v0

v1 whole, which is shorter than its diff:
```python
import functools
import types

import jax
import jax.numpy as jnp
from jax import lax
from jax.experimental import pallas as pl
from jax.experimental.pallas import tpu as pltpu
from jax.sharding import PartitionSpec as P

MESH = pl.DeviceIdType.MESH
HIGHEST = lax.Precision.HIGHEST
NB = 256
SIDE = 4
W = 256
NCH = 4
COPIES = 8
QUARTER = NB // SIDE


def dot(a, b):
    return jnp.dot(a, b, precision=HIGHEST, preferred_element_type=jnp.float32)


def bdot(a, b):
    return jnp.dot(a, b, preferred_element_type=jnp.float32)


def split(value):
    high = value.astype(jnp.bfloat16)
    return high, (value - high.astype(jnp.float32)).astype(jnp.bfloat16)


def few_rows(rows, wide):
    pair = jnp.concatenate([piece.astype(jnp.float32) for piece in split(rows)], axis=0).astype(jnp.bfloat16)
    product = sum(bdot(pair, piece) for piece in reversed(wide))
    return product[0:8] + product[8:16]


def rows_of(start, size):
    return pl.ds(pl.multiple_of(start, size), size)


def kernel(
    nz,
    m_hbm, l_hbm, linv_hbm, piv_hbm, w_hbm,
    out_ref, chk_ref,
    mat, contrib, owners, owners_b, linv, piv, w8, own_rows, lbuf, vbuf, usum,
    up1, t1s, v1s, up2, esend, slots,
    linv_high, linv_low, picks, places, factor_high, factor_low, rows_high, rows_low, wp_x, wp_y, sums_x, sums_y, totals,
    load_sem, mat_sem,
    su, ru, s2, r2, sd, rd,
    zs, zr, us, ur, cs, cr,
):
    prow, pcol = lax.axis_index("prow"), lax.axis_index("pcol")
    x, y = prow // SIDE, prow % SIDE
    z, core = pcol // 2, pcol % 2
    top = prow == 0

    x_peers = [(lax.rem(x + d, SIDE) * SIDE + y, pcol) for d in (1, 2, 3)]
    y_peers = [(x * SIDE + lax.rem(y + d, SIDE), pcol) for d in (1, 2, 3)]
    far_first = sorted(range(1, nz), key=lambda d: -min(d, nz - d))
    line = [lax.rem(z + d, nz) * 2 for d in far_first]
    z_peers = [(prow, column + 1) for column in line]
    plane_peers = [(lax.rem(prow + d, SIDE * SIDE), pcol) for d in range(1, SIDE * SIDE)]
    twin = (prow, z * 2 + 1 - core)

    w8[...] = jnp.zeros_like(w8)
    loads = [
        pltpu.make_async_copy(piv_hbm, piv, load_sem.at[0]),
        pltpu.make_async_copy(w_hbm, w8.at[pl.ds(0, 2)], load_sem.at[1]),
        pltpu.make_async_copy(l_hbm, own_rows, load_sem.at[2]),
        pltpu.make_async_copy(linv_hbm, linv, load_sem.at[3]),
    ]
    for copy in loads[:2]:
        copy.start()

    def chunk_cols(n):
        return pl.ds(pl.multiple_of((n % 2) * 2 * W + (n // 2) * W, W), W)

    def mat_load(n):
        cols = chunk_cols(n)
        return pltpu.make_async_copy(m_hbm.at[:, cols], mat.at[:, cols], mat_sem.at[n])

    for n in range(NCH):
        mat_load(n).start()
    for copy in loads[2:]:
        copy.start()

    barrier = pltpu.get_barrier_semaphore()

    def greet(peer):
        pl.semaphore_signal(barrier, inc=1, device_id=peer, device_id_type=MESH)

    for row, _ in x_peers + y_peers:
        greet((row, z * 2))

    @pl.when(core == 1)
    def _():
        greet(twin)
        for column in line:
            greet((prow, column + 1))

    def remote(src, dst, send_sem, recv_sem, peer):
        return pltpu.make_async_remote_copy(
            src_ref=src, dst_ref=dst, send_sem=send_sem, recv_sem=recv_sem,
            device_id=peer, device_id_type=MESH,
        )

    def begin(copies):
        for copy in copies:
            copy.start()

    def left(copies):
        for copy in copies:
            copy.wait_send()

    def landed(copies):
        for copy in copies:
            copy.wait_recv()

    def on(which):
        return pl.when(core == which)

    loads[0].wait()
    loads[1].wait()
    base = prow * NB
    row_ids = lax.broadcasted_iota(jnp.int32, (NB, NB), 0)
    lane_ids = lax.broadcasted_iota(jnp.int32, (NB, NB), 1)
    piv_cols = jnp.transpose(jnp.broadcast_to(piv[...], (NB, NB)))
    pick = jnp.where(piv_cols - base == lane_ids, 1.0, 0.0)
    picks[pl.ds(0, NB), :] = pick.astype(jnp.bfloat16)
    keep_row = 1.0 - jnp.sum(pick, axis=0, keepdims=True)
    kept = jnp.concatenate([piece.astype(jnp.float32) for piece in split(w8[...] * keep_row)], axis=0)
    picks[pl.ds(NB, 16), :] = kept.astype(jnp.bfloat16)

    def ring_of(half):
        a, b = (x, y) if half == 0 else (y, x)

        def place(a, b):
            return a * SIDE + b if half == 0 else b * SIDE + a

        outer = {d: lax.rem(a + d, SIDE) for d in (0, 1, 2, 3)}
        inner = {d: lax.rem(b + d, SIDE) for d in (1, 2, 3)}
        return types.SimpleNamespace(
            half=half, a=a, b=b, outer=outer, inner=inner,
            who={d: place(outer[d], b) for d in outer},
            to={d: (place(outer[d], b), pcol) for d in outer},
            to_inner={d: (place(a, inner[d]), pcol) for d in inner},
            rows={d: rows_of(outer[d] * QUARTER, QUARTER) for d in outer},
        )

    rings = ring_of(0), ring_of(1)

    def up_outer(n):
        r = rings[n % 2]
        return [
            remote(
                contrib.at[r.rows[d], chunk_cols(n)], up1.at[n, d - 1], su.at[n, d - 1], ru.at[n, d - 1], r.to[d])
            for d in (1, 2, 3)
        ]

    def inner(n):
        r = rings[n % 2]
        return [
            remote(
                v1s.at[n], up2.at[n, d - 1], s2.at[n, d - 1], r2.at[n, d - 1], r.to_inner[d])
            for d in (1, 2, 3)
        ]

    def down_outer(n):
        r = rings[n % 2]
        return [
            remote(
                esend.at[n, d - 1], slots.at[r.rows[0], chunk_cols(n)], sd.at[n, d - 1], rd.at[n, d - 1], r.to[d])
            for d in (1, 2, 3)
        ]

    wp_row, wp_column, wp = wp_x.at[x], wp_y.at[y], wp_x.at[SIDE]
    sums_row, sums_column = sums_x.at[x], sums_y.at[y]
    checked = vbuf.at[prow]
    rows_over = [remote(own_rows, lbuf.at[z, 0], zs.at[nz], zr.at[nz], twin)]
    z1 = [remote(lbuf.at[z], lbuf.at[z], zs.at[n], zr.at[n], peer) for n, peer in enumerate(z_peers)]
    z2 = [remote(lbuf, lbuf, zs.at[nz - 1], zr.at[nz - 1], twin)]
    c1 = [remote(wp_row, wp_row, cs.at[0, n], cr.at[0, n], peer) for n, peer in enumerate(x_peers)]
    c2 = [remote(wp_column, wp_column, cs.at[1, n], cr.at[1, n], peer) for n, peer in enumerate(y_peers)]
    wp_over = [remote(wp, wp, cs.at[4, 0], cr.at[4, 0], twin)]
    c3 = [remote(sums_row, sums_row, cs.at[2, n], cr.at[2, n], peer) for n, peer in enumerate(x_peers)]
    c4 = [remote(sums_column, sums_column, cs.at[3, n], cr.at[3, n], peer) for n, peer in enumerate(y_peers)]
    c5 = [remote(checked, checked, us.at[n], ur.at[n], peer) for n, peer in enumerate(plane_peers)]
    u_over = [remote(usum, usum, cs.at[4, 1], cr.at[4, 1], twin)]

    loads[2].wait()

    @on(0)
    def _():
        pl.semaphore_wait(barrier, 13)
        begin(rows_over)

    place = jnp.where(piv[...] - base == row_ids, 1.0, 0.0)


    for n in range(NCH):
        mat_load(n).wait()
        cols = chunk_cols(n)
        block = mat[:, cols]
        high = block.astype(jnp.bfloat16)
        middle = (block - high.astype(jnp.float32)).astype(jnp.bfloat16)
        picked = bdot(picks[...], middle) + bdot(picks[...], high)
        contrib[:, cols] = jnp.where(top, block, picked[0:NB])
        q = (n % 2) * 2 + n // 2
        sums_row[pl.ds(2 * q, 2), :] = picked[NB : NB + 2] + picked[NB + 8 : NB + 10]
        if n == 0:
            @on(1)
            def _():
                landed(rows_over)

        begin(up_outer(n))

        if n == 1:
            @on(0)
            def _():
                wp_row[...] = few_rows(w8[...], (place.astype(jnp.bfloat16),))
                begin(c1)


    @on(1)
    def _():
        lbuf[z, 1] = own_rows[...]
        pl.semaphore_wait(barrier, len(line))
        begin(z1)

    holders = piv_cols >> 8
    owners[...] = holders
    owners_b[0] = holders & (SIDE - 1)
    owners_b[1] = holders >> 2
    loads[3].wait()
    linv_high[...], linv_low[...] = split(linv[...])

    for n in range(NCH):
        r = rings[n % 2]
        landed(up_outer(n))
        rows = r.rows[0]
        who = owners[rows, :]
        p1 = t1 = contrib[rows, chunk_cols(n)]
        for d in (1, 2, 3):
            got = up1[n, d - 1]
            p1 = jnp.where(who == r.who[SIDE - d], got, p1)
            t1 = jnp.where(r.a == d, got, t1)
        passing = jnp.logical_and(owners_b[r.half, rows, :] != 0, r.b == 0)
        t1s[n] = t1
        v1s[n] = jnp.where(passing, t1, p1)
        begin(inner(n))

        if n == 1:
            @on(0)
            def _():
                landed(c1)
                wp_column[...] = ((wp_x[0] + wp_x[1]) + wp_x[2]) + wp_x[3]
                begin(c2)


    @on(0)
    def _():
        landed(c2)
        wp[...] = ((wp_y[0] + wp_y[1]) + wp_y[2]) + wp_y[3]
        begin(wp_over)

    keep_col = jnp.where(top, 0.0, 1.0 - jnp.sum(place, axis=1, keepdims=True))

    for n in range(NCH):
        r = rings[n % 2]
        landed(inner(n))
        rows = r.rows[0]
        who, who_b = owners[rows, :], owners_b[r.half, rows, :]
        p3, t3 = v1s[n], t1s[n]
        for d in (1, 2, 3):
            got = up2[n, d - 1]
            p3 = jnp.where(who_b == r.inner[SIDE - d], got, p3)
            t3 = jnp.where(r.b == d, got, t3)
        for d in (1, 2, 3):
            esend[n, d - 1] = jnp.where(who == r.who[d], t3, p3)
        slots[rows, chunk_cols(n)] = jnp.where(who == prow, t3, p3)
        begin(down_outer(n))

    @on(1)
    def _():
        landed(z1)
        begin(z2)

    @on(1)
    def _():
        landed(wp_over)

    @pl.when(top)
    def _():
        for q in range(4):
            part = few_rows(wp[...], split(mat[:, pl.ds(q * W, W)]))
            sums_row[pl.ds(2 * q, 2), :] = part[0:2]

    begin(c3)

    for n in range(NCH):
        left(up_outer(n))
        left(inner(n))

    @on(0)
    def _():
        landed(z2)

    lower_high, lower_low = split(jnp.where(top, jnp.where(row_ids == lane_ids, -1.0, 0.0), lbuf[...].reshape(NB, NB)))

    @on(1)
    def _():
        checked[...] = few_rows(w8[...], (lower_high, lower_low))[0:2]
        begin(c5)

    multiplier = -(
        (bdot(lower_low, linv_high[...]) + bdot(lower_high, linv_low[...])) + bdot(lower_high, linv_high[...])
    )
    factor_high[...], factor_low[...] = split(multiplier)
    places[...] = place.astype(jnp.bfloat16)
    landed(c3)
    sums_column[...] = ((sums_x[0] + sums_x[1]) + sums_x[2]) + sums_x[3]
    begin(c4)

    for n in range(NCH):
        landed(down_outer(n))
        cols = chunk_cols(n)
        got = slots[:, cols]
        got_high, got_low = split(got)
        high, low_part = split(jnp.where(owners[...] == prow, contrib[:, cols], got))
        rows_high[:, cols] = high
        rows_low[:, cols] = low_part
        product = (bdot(factor_low[...], high) + bdot(factor_high[...], low_part)) + bdot(factor_high[...], high)
        landing = bdot(places[...], got_low) + bdot(places[...], got_high)
        out_ref[:, cols] = (mat[:, cols] * keep_col + landing) + product

    @on(1)
    def _():
        landed(c5)
        usum[...] = jnp.sum(vbuf[...], axis=0)
        begin(u_over)
        left(z1 + z2 + c5)

    @on(0)
    def _():
        left(rows_over + c1 + c2 + wp_over)
        landed(u_over)

    left(c3)
    for n in range(NCH):
        left(down_outer(n))

    landed(c4)
    left(c4)
    totals[...] = ((sums_y[0] + sums_y[1]) + sums_y[2]) + sums_y[3]
    u = jnp.concatenate([usum[...], jnp.zeros((6, NB), jnp.float32)], axis=0)
    check_factor = -few_rows(u, (linv_high[...], linv_low[...]))
    for q in range(NCH):
        cols = pl.ds(q * W, W)
        added = few_rows(check_factor, (rows_high[:, cols], rows_low[:, cols]))
        chk_ref[:, cols] = added[0:2] + totals[pl.ds(2 * q, 2), :]

    @on(1)
    def _():
        left(u_over)


def hand_over(updated, checks, updated_out, checks_out, sems):
    size = NB // COPIES
    parts = [pl.ds(k * size, size) for k in range(COPIES)]
    copies = [pltpu.make_async_copy(updated.at[p], updated_out.at[p], sems.at[k]) for k, p in enumerate(parts)]
    copies.append(pltpu.make_async_copy(checks, checks_out, sems.at[COPIES]))
    for copy in copies:
        copy.start()
    for copy in copies:
        copy.wait()


def shards(nz, matrix, lpanel, linv, pivots, weights):
    f32 = jnp.float32
    columns = matrix.shape[1]
    n = NCH
    anywhere = pl.BlockSpec(memory_space=pl.ANY)
    vmem = pltpu.VMEM
    dma = pltpu.SemaphoreType.DMA
    operands = (matrix, lpanel, linv, pivots.reshape(1, NB), weights)
    updated, checks = pl.pallas_call(
        functools.partial(kernel, nz),
        out_shape=(vmem((NB, columns), f32), vmem((2, columns), f32)),
        in_specs=[anywhere] * 5,
        out_specs=(pl.BlockSpec(memory_space=vmem), pl.BlockSpec(memory_space=vmem)),
        scratch_shapes=[
            vmem((NB, columns), f32),
            vmem((NB, columns), f32),
            vmem((NB, NB), jnp.int32),
            vmem((2, NB, NB), jnp.int32),
            vmem((NB, NB), f32),
            vmem((1, NB), jnp.int32),
            vmem((8, NB), f32),
            vmem((8, NB), f32),
            vmem((nz, 2, 8, NB), f32),
            vmem((SIDE * SIDE, 2, NB), f32),
            vmem((2, NB), f32),
            vmem((n, 3, QUARTER, W), f32),
            vmem((n, QUARTER, W), f32),
            vmem((n, QUARTER, W), f32),
            vmem((n, 3, QUARTER, W), f32),
            vmem((n, 3, QUARTER, W), f32),
            vmem((NB, columns), f32),
            vmem((NB, NB), jnp.bfloat16),
            vmem((NB, NB), jnp.bfloat16),
            vmem((NB + 16, NB), jnp.bfloat16),
            vmem((NB, NB), jnp.bfloat16),
            vmem((NB, NB), jnp.bfloat16),
            vmem((NB, NB), jnp.bfloat16),
            vmem((NB, columns), jnp.bfloat16),
            vmem((NB, columns), jnp.bfloat16),
            vmem((5, 8, NB), f32),
            vmem((4, 8, NB), f32),
            vmem((4, 8, W), f32),
            vmem((4, 8, W), f32),
            vmem((8, W), f32),
            dma((4,)),
            dma((n,)),
            dma((n, 3)), dma((n, 3)), dma((n, 3)), dma((n, 3)), dma((n, 3)), dma((n, 3)),
            dma((nz + 1,)), dma((nz + 1,)), dma((SIDE * SIDE - 1,)), dma((SIDE * SIDE - 1,)),
            dma((5, 3)), dma((5, 3)),
        ],
        compiler_params=pltpu.CompilerParams(
            collective_id=0, has_side_effects=True, vmem_limit_bytes=40 * 1024 * 1024
        ),
        cost_estimate=pl.CostEstimate(flops=500_000_000, bytes_accessed=4_000_000, transcendentals=0),
    )(*[pltpu.with_memory_space_constraint(v, pltpu.HBM) for v in operands])
    return pl.pallas_call(
        hand_over,
        out_shape=(
            jax.ShapeDtypeStruct((NB, columns), f32),
            jax.ShapeDtypeStruct((2, columns), f32),
        ),
        in_specs=[anywhere] * 2,
        out_specs=(anywhere, anywhere),
        scratch_shapes=[dma((COPIES + 1,))],
        cost_estimate=pl.CostEstimate(flops=0, bytes_accessed=2_000_000, transcendentals=0),
    )(*[pltpu.with_memory_space_constraint(v, vmem) for v in (updated, checks)])


def solution(mesh):
    return jax.shard_map(
        functools.partial(shards, mesh.shape["pcol"] // 2),
        mesh=mesh,
        in_specs=(P("prow", "pcol"), P(("prow", "pcol"), None), P(), P(), P(None, "prow")),
        out_specs=(P("prow", "pcol"), P(None, "pcol")),
        check_vma=False,
    )
```

time: 196 us -> 37.4 us (0.19)
  the two profiles are of different devices: /device:TPU:32 before, /device:TPU:1 now
where the time goes in v1:
time: 37.4 us; the launch traced here: 37.3 us
  Pallas kernels  36.6 us (98%)
  between operations  0.64 us (2%)
    pallas_call x1, Pallas kernels, shards(): pl.pallas_call(functools.partial(kernel, nz), out_shape=(vmem((NB, column...  35.6 us
    pallas_call x1, Pallas kernels, shards(): pl.pallas_call(hand_over, out_shape=(jax.ShapeDtypeStruct((NB, columns),...  1.04 us

profile of v1, /device:TPU:1, one launch (start us, length us, event | category | flops | bytes accessed | tf_op | source)
XLA Modules:
  0.0 37.3 jit_solution(12194078509084049737)
XLA Ops:
  0.6 35.6 %shard_map.68 = (f32[256,1024]{1,0:T(8,128)S(1)}, f32[2,1024]{1,0:T(2,128)S(1)}) custom-call(f32[256,1024]{1,0:T(8,128)} %m_hbm.1, f32[8,256]{1,0:T(8,128)} %l_hbm.1, f32[256,256]{1,0:T(8,128)} %linv_hbm.1, s32[1,256]{1,0:T(1,128)} %bitcast.1, f32[2,256]{1,0:T(2,128)} %w_hbm.1), custom_call_target="tpu_custom_call" | custom-call | flops 500000000 | bytes 4000000 | tf_op jit(solution)/shard_map/pallas_call | solution.py:389
  36.2 1.0 %shard_map.69 = (f32[256,1024]{1,0:T(8,128)}, f32[2,1024]{1,0:T(2,128)}) custom-call(f32[256,1024]{1,0:T(8,128)S(1)} %get-tuple-element.4.updated, f32[2,1024]{1,0:T(2,128)S(1)} %get-tuple-element.5.checks), custom_call_target="tpu_custom_call" | custom-call | bytes 2000000 | tf_op jit(solution)/shard_map/pallas_call | solution.py:436

commit v2 on v1

--- a/solution.py
+++ b/solution.py
@@ -15,6 +15,7 @@
 W = 256
 NCH = 4
 COPIES = 8
+PAIRS = ((0, 1), (2, 3))
 QUARTER = NB // SIDE
 
 
@@ -47,10 +48,10 @@
     out_ref, chk_ref,
     mat, contrib, owners, owners_b, linv, piv, w8, own_rows, lbuf, vbuf, usum,
     up1, t1s, v1s, up2, esend, slots,
-    linv_high, linv_low, picks, places, factor_high, factor_low, rows_high, rows_low, wp_x, wp_y, sums_x, sums_y, totals,
+    linv_high, linv_low, picks, places, factor_high, factor_low, rows_high, rows_low, given, gathered, totals,
     load_sem, mat_sem,
     su, ru, s2, r2, sd, rd,
-    zs, zr, us, ur, cs, cr,
+    zs, zr, us, ur, ts, tr,
 ):
     prow, pcol = lax.axis_index("prow"), lax.axis_index("pcol")
     x, y = prow // SIDE, prow % SIDE
@@ -176,19 +177,15 @@
             for d in (1, 2, 3)
         ]
 
-    wp_row, wp_column, wp = wp_x.at[x], wp_y.at[y], wp_x.at[SIDE]
-    sums_row, sums_column = sums_x.at[x], sums_y.at[y]
     checked = vbuf.at[prow]
     rows_over = [remote(own_rows, lbuf.at[z, 0], zs.at[nz], zr.at[nz], twin)]
     z1 = [remote(lbuf.at[z], lbuf.at[z], zs.at[n], zr.at[n], peer) for n, peer in enumerate(z_peers)]
     z2 = [remote(lbuf, lbuf, zs.at[nz - 1], zr.at[nz - 1], twin)]
-    c1 = [remote(wp_row, wp_row, cs.at[0, n], cr.at[0, n], peer) for n, peer in enumerate(x_peers)]
-    c2 = [remote(wp_column, wp_column, cs.at[1, n], cr.at[1, n], peer) for n, peer in enumerate(y_peers)]
-    wp_over = [remote(wp, wp, cs.at[4, 0], cr.at[4, 0], twin)]
-    c3 = [remote(sums_row, sums_row, cs.at[2, n], cr.at[2, n], peer) for n, peer in enumerate(x_peers)]
-    c4 = [remote(sums_column, sums_column, cs.at[3, n], cr.at[3, n], peer) for n, peer in enumerate(y_peers)]
+    to_top = [remote(given, gathered.at[prow], ts.at[0], tr.at[lax.rem(prow + 15, 16)], (0, pcol))]
+    at_top = [remote(given, gathered.at[k], ts.at[0], tr.at[k - 1], (0, pcol)) for k in range(1, SIDE * SIDE)]
+    from_top = [remote(totals, totals, ts.at[k], tr.at[SIDE * SIDE - 1], (k, pcol)) for k in range(1, SIDE * SIDE)]
     c5 = [remote(checked, checked, us.at[n], ur.at[n], peer) for n, peer in enumerate(plane_peers)]
-    u_over = [remote(usum, usum, cs.at[4, 1], cr.at[4, 1], twin)]
+    u_over = [remote(usum, usum, ts.at[SIDE * SIDE], tr.at[SIDE * SIDE], twin)]
 
     loads[2].wait()
 
@@ -200,29 +197,24 @@
     place = jnp.where(piv[...] - base == row_ids, 1.0, 0.0)
 
 
-    for n in range(NCH):
-        mat_load(n).wait()
-        cols = chunk_cols(n)
-        block = mat[:, cols]
-        high = block.astype(jnp.bfloat16)
-        middle = (block - high.astype(jnp.float32)).astype(jnp.bfloat16)
-        picked = bdot(picks[...], middle) + bdot(picks[...], high)
-        contrib[:, cols] = jnp.where(top, block, picked[0:NB])
-        q = (n % 2) * 2 + n // 2
-        sums_row[pl.ds(2 * q, 2), :] = picked[NB : NB + 2] + picked[NB + 8 : NB + 10]
-        if n == 0:
+    for pair in PAIRS:
+        for n in pair:
+            mat_load(n).wait()
+        for n in pair:
+            cols = chunk_cols(n)
+            block = mat[:, cols]
+            high, middle = split(block)
+            picked = bdot(picks[...], middle) + bdot(picks[...], high)
+            contrib[:, cols] = jnp.where(top, block, picked[0:NB])
+            q = (n % 2) * 2 + n // 2
+            given[pl.ds(2 * q, 2), :] = picked[NB : NB + 2] + picked[NB + 8 : NB + 10]
+        if pair == PAIRS[0]:
             @on(1)
             def _():
                 landed(rows_over)
 
-        begin(up_outer(n))
-
-        if n == 1:
-            @on(0)
-            def _():
-                wp_row[...] = few_rows(w8[...], (place.astype(jnp.bfloat16),))
-                begin(c1)
-
+        for n in pair:
+            begin(up_outer(n))
 
     @on(1)
     def _():
@@ -252,19 +244,10 @@
         v1s[n] = jnp.where(passing, t1, p1)
         begin(inner(n))
 
-        if n == 1:
-            @on(0)
-            def _():
-                landed(c1)
-                wp_column[...] = ((wp_x[0] + wp_x[1]) + wp_x[2]) + wp_x[3]
-                begin(c2)
-
-
-    @on(0)
-    def _():
-        landed(c2)
-        wp[...] = ((wp_y[0] + wp_y[1]) + wp_y[2]) + wp_y[3]
-        begin(wp_over)
+    @pl.when(prow != 0)
+    def _():
+        given[pl.ds(8, 8), :] = few_rows(w8[...], (place.astype(jnp.bfloat16),))
+        begin(to_top)
 
     keep_col = jnp.where(top, 0.0, 1.0 - jnp.sum(place, axis=1, keepdims=True))
 
@@ -288,17 +271,15 @@
         landed(z1)
         begin(z2)
 
-    @on(1)
-    def _():
-        landed(wp_over)
-
     @pl.when(top)
     def _():
-        for q in range(4):
-            part = few_rows(wp[...], split(mat[:, pl.ds(q * W, W)]))
-            sums_row[pl.ds(2 * q, 2), :] = part[0:2]
-
-    begin(c3)
+        landed(at_top)
+        added = jnp.sum(gathered[1:], axis=0)
+        totals[...] = added[0:8]
+        part = few_rows(added[8:16], split(mat[...]))
+        for q in range(NCH):
+            totals[pl.ds(2 * q, 2), :] = totals[pl.ds(2 * q, 2), :] + part[0:2, q * W : (q + 1) * W]
+        begin(from_top)
 
     for n in range(NCH):
         left(up_outer(n))
@@ -320,47 +301,55 @@
     )
     factor_high[...], factor_low[...] = split(multiplier)
     places[...] = place.astype(jnp.bfloat16)
-    landed(c3)
-    sums_column[...] = ((sums_x[0] + sums_x[1]) + sums_x[2]) + sums_x[3]
-    begin(c4)
-
-    for n in range(NCH):
-        landed(down_outer(n))
-        cols = chunk_cols(n)
-        got = slots[:, cols]
-        got_high, got_low = split(got)
-        high, low_part = split(jnp.where(owners[...] == prow, contrib[:, cols], got))
-        rows_high[:, cols] = high
-        rows_low[:, cols] = low_part
-        product = (bdot(factor_low[...], high) + bdot(factor_high[...], low_part)) + bdot(factor_high[...], high)
-        landing = bdot(places[...], got_low) + bdot(places[...], got_high)
-        out_ref[:, cols] = (mat[:, cols] * keep_col + landing) + product
-
-    @on(1)
-    def _():
-        landed(c5)
-        usum[...] = jnp.sum(vbuf[...], axis=0)
-        begin(u_over)
-        left(z1 + z2 + c5)
-
-    @on(0)
-    def _():
-        left(rows_over + c1 + c2 + wp_over)
-        landed(u_over)
-
-    left(c3)
+
+    for pair in PAIRS:
+        for n in pair:
+            landed(down_outer(n))
+        for n in pair:
+            cols = chunk_cols(n)
+            got = slots[:, cols]
+            got_high, got_low = split(got)
+            high, low_part = split(jnp.where(owners[...] == prow, contrib[:, cols], got))
+            rows_high[:, cols] = high
+            rows_low[:, cols] = low_part
+            product = (bdot(factor_low[...], high) + bdot(factor_high[...], low_part)) + bdot(factor_high[...], high)
+            landing = bdot(places[...], got_low) + bdot(places[...], got_high)
+            out_ref[:, cols] = (mat[:, cols] * keep_col + landing) + product
+        if pair == PAIRS[0]:
+            @on(1)
+            def _():
+                landed(c5)
+                usum[...] = jnp.sum(vbuf[...], axis=0)
+                begin(u_over)
+
     for n in range(NCH):
         left(down_outer(n))
 
-    landed(c4)
-    left(c4)
-    totals[...] = ((sums_y[0] + sums_y[1]) + sums_y[2]) + sums_y[3]
+    @on(1)
+    def _():
+        left(z1 + z2 + c5)
+
+    @on(0)
+    def _():
+        left(rows_over)
+        landed(u_over)
+
     u = jnp.concatenate([usum[...], jnp.zeros((6, NB), jnp.float32)], axis=0)
     check_factor = -few_rows(u, (linv_high[...], linv_low[...]))
+
+    @pl.when(prow != 0)
+    def _():
+        landed(from_top[:1])
+        left(to_top)
+
+    @pl.when(top)
+    def _():
+        left(from_top)
+
+    checked_rows = few_rows(check_factor, (rows_high[...], rows_low[...]))
     for q in range(NCH):
         cols = pl.ds(q * W, W)
-        added = few_rows(check_factor, (rows_high[:, cols], rows_low[:, cols]))
-        chk_ref[:, cols] = added[0:2] + totals[pl.ds(2 * q, 2), :]
+        chk_ref[:, cols] = checked_rows[0:2, q * W : (q + 1) * W] + totals[pl.ds(2 * q, 2), :]
 
     @on(1)
     def _():
@@ -417,16 +406,14 @@
             vmem((NB, NB), jnp.bfloat16),
             vmem((NB, columns), jnp.bfloat16),
             vmem((NB, columns), jnp.bfloat16),
-            vmem((5, 8, NB), f32),
-            vmem((4, 8, NB), f32),
-            vmem((4, 8, W), f32),
-            vmem((4, 8, W), f32),
+            vmem((16, W), f32),
+            vmem((SIDE * SIDE, 16, W), f32),
             vmem((8, W), f32),
             dma((4,)),
             dma((n,)),
             dma((n, 3)), dma((n, 3)), dma((n, 3)), dma((n, 3)), dma((n, 3)), dma((n, 3)),
             dma((nz + 1,)), dma((nz + 1,)), dma((SIDE * SIDE - 1,)), dma((SIDE * SIDE - 1,)),
-            dma((5, 3)), dma((5, 3)),
+            dma((SIDE * SIDE + 1,)), dma((SIDE * SIDE + 1,)),
         ],
         compiler_params=pltpu.CompilerParams(
             collective_id=0, has_side_effects=True, vmem_limit_bytes=40 * 1024 * 1024

time: 37.4 us -> 36.8 us (0.984)
  Pallas kernels: 36.6 us -> 36.1 us
    pallas_call x1, Pallas kernels: 35.6 us -> 35 us  [shards(): pl.pallas_call(functools.partial(kernel, nz), out_shape=(vmem((NB, column...]
where the time goes in v2:
time: 36.8 us; the launch traced here: 36.7 us
  Pallas kernels  36.1 us (98%)
  between operations  0.64 us (2%)
    pallas_call x1, Pallas kernels, shards(): pl.pallas_call(functools.partial(kernel, nz), out_shape=(vmem((NB, column...  35 us
    pallas_call x1, Pallas kernels, shards(): pl.pallas_call(hand_over, out_shape=(jax.ShapeDtypeStruct((NB, columns),...  1.04 us

profile of v2, /device:TPU:1, one launch (start us, length us, event | category | flops | bytes accessed | tf_op | source)
XLA Modules:
  0.0 36.7 jit_solution(2707282629074117256)
XLA Ops:
  0.6 35.0 %shard_map.68 = (f32[256,1024]{1,0:T(8,128)S(1)}, f32[2,1024]{1,0:T(2,128)S(1)}) custom-call(f32[256,1024]{1,0:T(8,128)} %m_hbm.1, f32[8,256]{1,0:T(8,128)} %l_hbm.1, f32[256,256]{1,0:T(8,128)} %linv_hbm.1, s32[1,256]{1,0:T(1,128)} %bitcast.1, f32[2,256]{1,0:T(2,128)} %w_hbm.1), custom_call_target="tpu_custom_call" | custom-call | flops 500000000 | bytes 4000000 | tf_op jit(solution)/shard_map/pallas_call | solution.py:378
  35.7 1.0 %shard_map.69 = (f32[256,1024]{1,0:T(8,128)}, f32[2,1024]{1,0:T(2,128)}) custom-call(f32[256,1024]{1,0:T(8,128)S(1)} %get-tuple-element.4.updated, f32[2,1024]{1,0:T(2,128)S(1)} %get-tuple-element.5.checks), custom_call_target="tpu_custom_call" | custom-call | bytes 2000000 | tf_op jit(solution)/shard_map/pallas_call | solution.py:423

commit v3 on v2

--- a/solution.py
+++ b/solution.py
@@ -46,12 +46,11 @@
     nz,
     m_hbm, l_hbm, linv_hbm, piv_hbm, w_hbm,
     out_ref, chk_ref,
-    mat, contrib, owners, owners_b, linv, piv, w8, own_rows, lbuf, vbuf, usum,
+    mat, contrib, owners, owners_b, linv, piv, w8, own_rows, lbuf, vbuf,
     up1, t1s, v1s, up2, esend, slots,
-    linv_high, linv_low, picks, places, factor_high, factor_low, rows_high, rows_low, given, gathered, totals,
+    linv_high, linv_low, picks, places, factor_high, factor_low, rows_high, rows_low, given, gathered, sums, totals,
     load_sem, mat_sem,
-    su, ru, s2, r2, sd, rd,
-    zs, zr, us, ur, ts, tr,
+    ru, r2, rd, ss, rs,
 ):
     prow, pcol = lax.axis_index("prow"), lax.axis_index("pcol")
     x, y = prow // SIDE, prow % SIDE
@@ -112,13 +111,8 @@
         for copy in copies:
             copy.start()
 
-    def left(copies):
-        for copy in copies:
-            copy.wait_send()
-
-    def landed(copies):
-        for copy in copies:
-            copy.wait_recv()
+    def done(ref, sem):
+        pltpu.make_async_copy(ref, ref, sem).wait()
 
     def on(which):
         return pl.when(core == which)
@@ -157,7 +151,7 @@
         r = rings[n % 2]
         return [
             remote(
-                contrib.at[r.rows[d], chunk_cols(n)], up1.at[n, d - 1], su.at[n, d - 1], ru.at[n, d - 1], r.to[d])
+                contrib.at[r.rows[d], chunk_cols(n)], up1.at[n, d - 1], ss.at[0], ru.at[n], r.to[d])
             for d in (1, 2, 3)
         ]
 
@@ -165,7 +159,7 @@
         r = rings[n % 2]
         return [
             remote(
-                v1s.at[n], up2.at[n, d - 1], s2.at[n, d - 1], r2.at[n, d - 1], r.to_inner[d])
+                v1s.at[n], up2.at[n, d - 1], ss.at[1], r2.at[n], r.to_inner[d])
             for d in (1, 2, 3)
         ]
 
@@ -173,19 +167,17 @@
         r = rings[n % 2]
         return [
             remote(
-                esend.at[n, d - 1], slots.at[r.rows[0], chunk_cols(n)], sd.at[n, d - 1], rd.at[n, d - 1], r.to[d])
+                esend.at[n, d - 1], slots.at[r.rows[0], chunk_cols(n)], ss.at[2], rd.at[n], r.to[d])
             for d in (1, 2, 3)
         ]
 
-    checked = vbuf.at[prow]
-    rows_over = [remote(own_rows, lbuf.at[z, 0], zs.at[nz], zr.at[nz], twin)]
-    z1 = [remote(lbuf.at[z], lbuf.at[z], zs.at[n], zr.at[n], peer) for n, peer in enumerate(z_peers)]
-    z2 = [remote(lbuf, lbuf, zs.at[nz - 1], zr.at[nz - 1], twin)]
-    to_top = [remote(given, gathered.at[prow], ts.at[0], tr.at[lax.rem(prow + 15, 16)], (0, pcol))]
-    at_top = [remote(given, gathered.at[k], ts.at[0], tr.at[k - 1], (0, pcol)) for k in range(1, SIDE * SIDE)]
-    from_top = [remote(totals, totals, ts.at[k], tr.at[SIDE * SIDE - 1], (k, pcol)) for k in range(1, SIDE * SIDE)]
-    c5 = [remote(checked, checked, us.at[n], ur.at[n], peer) for n, peer in enumerate(plane_peers)]
-    u_over = [remote(usum, usum, ts.at[SIDE * SIDE], tr.at[SIDE * SIDE], twin)]
+    checked, kept_here = vbuf.at[prow], sums.at[prow]
+    rows_over = [remote(own_rows, lbuf.at[z, 0], ss.at[3], rs.at[3], twin)]
+    z1 = [remote(lbuf.at[z], lbuf.at[z], ss.at[4], rs.at[4], peer) for peer in z_peers]
+    z2 = [remote(lbuf, lbuf, ss.at[5], rs.at[5], twin)]
+    to_top = [remote(given, gathered.at[prow], ss.at[6], rs.at[6], (0, pcol))]
+    shared = [remote(kept_here, kept_here, ss.at[7], rs.at[7], peer) for peer in plane_peers]
+    c5 = [remote(checked, checked, ss.at[8], rs.at[8], peer) for peer in plane_peers]
 
     loads[2].wait()
 
@@ -207,11 +199,11 @@
             picked = bdot(picks[...], middle) + bdot(picks[...], high)
             contrib[:, cols] = jnp.where(top, block, picked[0:NB])
             q = (n % 2) * 2 + n // 2
-            given[pl.ds(2 * q, 2), :] = picked[NB : NB + 2] + picked[NB + 8 : NB + 10]
+            kept_here[pl.ds(2 * q, 2), :] = picked[NB : NB + 2] + picked[NB + 8 : NB + 10]
         if pair == PAIRS[0]:
             @on(1)
             def _():
-                landed(rows_over)
+                done(own_rows, rs.at[3])
 
         for n in pair:
             begin(up_outer(n))
@@ -231,7 +223,7 @@
 
     for n in range(NCH):
         r = rings[n % 2]
-        landed(up_outer(n))
+        done(up1.at[n], ru.at[n])
         rows = r.rows[0]
         who = owners[rows, :]
         p1 = t1 = contrib[rows, chunk_cols(n)]
@@ -246,14 +238,14 @@
 
     @pl.when(prow != 0)
     def _():
-        given[pl.ds(8, 8), :] = few_rows(w8[...], (place.astype(jnp.bfloat16),))
+        given[...] = few_rows(w8[...], (place.astype(jnp.bfloat16),))
         begin(to_top)
 
     keep_col = jnp.where(top, 0.0, 1.0 - jnp.sum(place, axis=1, keepdims=True))
 
     for n in range(NCH):
         r = rings[n % 2]
-        landed(inner(n))
+        done(up2.at[n], r2.at[n])
         rows = r.rows[0]
         who, who_b = owners[rows, :], owners_b[r.half, rows, :]
         p3, t3 = v1s[n], t1s[n]
@@ -266,36 +258,28 @@
         slots[rows, chunk_cols(n)] = jnp.where(who == prow, t3, p3)
         begin(down_outer(n))
 
+    @pl.when(top)
+    def _():
+        done(gathered.at[1:], rs.at[6])
+        part = few_rows(jnp.sum(gathered[1:], axis=0), split(mat[...]))
+        for q in range(NCH):
+            kept_here[pl.ds(2 * q, 2), :] = part[0:2, q * W : (q + 1) * W]
+
+    begin(shared)
+
     @on(1)
     def _():
-        landed(z1)
+        done(lbuf.at[1:], rs.at[4])
         begin(z2)
 
-    @pl.when(top)
-    def _():
-        landed(at_top)
-        added = jnp.sum(gathered[1:], axis=0)
-        totals[...] = added[0:8]
-        part = few_rows(added[8:16], split(mat[...]))
-        for q in range(NCH):
-            totals[pl.ds(2 * q, 2), :] = totals[pl.ds(2 * q, 2), :] + part[0:2, q * W : (q + 1) * W]
-        begin(from_top)
-
-    for n in range(NCH):
-        left(up_outer(n))
-        left(inner(n))
-
     @on(0)
     def _():
-        landed(z2)
+        done(lbuf, rs.at[5])
 
     lower_high, lower_low = split(jnp.where(top, jnp.where(row_ids == lane_ids, -1.0, 0.0), lbuf[...].reshape(NB, NB)))
 
-    @on(1)
-    def _():
-        checked[...] = few_rows(w8[...], (lower_high, lower_low))[0:2]
-        begin(c5)
-
+    checked[...] = few_rows(w8[...], (lower_high, lower_low))[0:2]
+    begin(c5)
     multiplier = -(
         (bdot(lower_low, linv_high[...]) + bdot(lower_high, linv_low[...])) + bdot(lower_high, linv_high[...])
     )
@@ -304,7 +288,7 @@
 
     for pair in PAIRS:
         for n in pair:
-            landed(down_outer(n))
+            done(esend.at[n], rd.at[n])
         for n in pair:
             cols = chunk_cols(n)
             got = slots[:, cols]
@@ -315,45 +299,36 @@
             product = (bdot(factor_low[...], high) + bdot(factor_high[...], low_part)) + bdot(factor_high[...], high)
             landing = bdot(places[...], got_low) + bdot(places[...], got_high)
             out_ref[:, cols] = (mat[:, cols] * keep_col + landing) + product
-        if pair == PAIRS[0]:
-            @on(1)
-            def _():
-                landed(c5)
-                usum[...] = jnp.sum(vbuf[...], axis=0)
-                begin(u_over)
-
-    for n in range(NCH):
-        left(down_outer(n))
-
-    @on(1)
-    def _():
-        left(z1 + z2 + c5)
-
-    @on(0)
-    def _():
-        left(rows_over)
-        landed(u_over)
-
-    u = jnp.concatenate([usum[...], jnp.zeros((6, NB), jnp.float32)], axis=0)
+
+    done(vbuf.at[1:], rs.at[8])
+    u = jnp.concatenate([jnp.sum(vbuf[...], axis=0), jnp.zeros((6, NB), jnp.float32)], axis=0)
     check_factor = -few_rows(u, (linv_high[...], linv_low[...]))
 
-    @pl.when(prow != 0)
-    def _():
-        landed(from_top[:1])
-        left(to_top)
-
-    @pl.when(top)
-    def _():
-        left(from_top)
-
+    done(sums.at[1:], rs.at[7])
+    totals[...] = jnp.sum(sums[...], axis=0)
     checked_rows = few_rows(check_factor, (rows_high[...], rows_low[...]))
     for q in range(NCH):
         cols = pl.ds(q * W, W)
         chk_ref[:, cols] = checked_rows[0:2, q * W : (q + 1) * W] + totals[pl.ds(2 * q, 2), :]
 
+    done(up1, ss.at[0])
+    done(up2, ss.at[1])
+    done(esend, ss.at[2])
+    done(sums.at[1:], ss.at[7])
+    done(vbuf.at[1:], ss.at[8])
+
+    @on(0)
+    def _():
+        done(own_rows, ss.at[3])
+
     @on(1)
     def _():
-        left(u_over)
+        done(lbuf.at[1:], ss.at[4])
+        done(lbuf, ss.at[5])
+
+    @pl.when(prow != 0)
+    def _():
+        done(given, ss.at[6])
 
 
 def hand_over(updated, checks, updated_out, checks_out, sems):
@@ -391,7 +366,6 @@
             vmem((8, NB), f32),
             vmem((nz, 2, 8, NB), f32),
             vmem((SIDE * SIDE, 2, NB), f32),
-            vmem((2, NB), f32),
             vmem((n, 3, QUARTER, W), f32),
             vmem((n, QUARTER, W), f32),
             vmem((n, QUARTER, W), f32),
@@ -406,14 +380,14 @@
             vmem((NB, NB), jnp.bfloat16),
             vmem((NB, columns), jnp.bfloat16),
             vmem((NB, columns), jnp.bfloat16),
-            vmem((16, W), f32),
-            vmem((SIDE * SIDE, 16, W), f32),
+            vmem((8, NB), f32),
+            vmem((SIDE * SIDE, 8, NB), f32),
+            vmem((SIDE * SIDE, 8, W), f32),
             vmem((8, W), f32),
             dma((4,)),
             dma((n,)),
-            dma((n, 3)), dma((n, 3)), dma((n, 3)), dma((n, 3)), dma((n, 3)), dma((n, 3)),
-            dma((nz + 1,)), dma((nz + 1,)), dma((SIDE * SIDE - 1,)), dma((SIDE * SIDE - 1,)),
-            dma((SIDE * SIDE + 1,)), dma((SIDE * SIDE + 1,)),
+            dma((n,)), dma((n,)), dma((n,)),
+            dma((9,)), dma((9,)),
         ],
         compiler_params=pltpu.CompilerParams(
             collective_id=0, has_side_effects=True, vmem_limit_bytes=40 * 1024 * 1024

time: 36.8 us -> 36.1 us (0.981)
  Pallas kernels: 36.1 us -> 35.3 us
    pallas_call x1, Pallas kernels: 35 us -> 34.3 us  [shards(): pl.pallas_call(functools.partial(kernel, nz), out_shape=(vmem((NB, column...]
where the time goes in v3:
time: 36.1 us; the launch traced here: 36 us
  Pallas kernels  35.3 us (98%)
  between operations  0.64 us (2%)
    pallas_call x1, Pallas kernels, shards(): pl.pallas_call(functools.partial(kernel, nz), out_shape=(vmem((NB, column...  34.3 us
    pallas_call x1, Pallas kernels, shards(): pl.pallas_call(hand_over, out_shape=(jax.ShapeDtypeStruct((NB, columns),...  1.04 us

profile of v3, /device:TPU:1, one launch (start us, length us, event | category | flops | bytes accessed | tf_op | source)
XLA Modules:
  0.0 36.0 jit_solution(14251638566317031152)
XLA Ops:
  0.6 34.3 %shard_map.68 = (f32[256,1024]{1,0:T(8,128)S(1)}, f32[2,1024]{1,0:T(2,128)S(1)}) custom-call(f32[256,1024]{1,0:T(8,128)} %m_hbm.1, f32[8,256]{1,0:T(8,128)} %l_hbm.1, f32[256,256]{1,0:T(8,128)} %linv_hbm.1, s32[1,256]{1,0:T(1,128)} %bitcast.1, f32[2,256]{1,0:T(2,128)} %w_hbm.1), custom_call_target="tpu_custom_call" | custom-call | flops 500000000 | bytes 4000000 | tf_op jit(solution)/shard_map/pallas_call | solution.py:353
  34.9 1.0 %shard_map.69 = (f32[256,1024]{1,0:T(8,128)}, f32[2,1024]{1,0:T(2,128)}) custom-call(f32[256,1024]{1,0:T(8,128)S(1)} %get-tuple-element.4.updated, f32[2,1024]{1,0:T(2,128)S(1)} %get-tuple-element.5.checks), custom_call_target="tpu_custom_call" | custom-call | bytes 2000000 | tf_op jit(solution)/shard_map/pallas_call | solution.py:397

commit v4 on v3

--- a/solution.py
+++ b/solution.py
@@ -14,7 +14,7 @@
 SIDE = 4
 W = 256
 NCH = 4
-COPIES = 8
+COPIES = 2
 PAIRS = ((0, 1), (2, 3))
 QUARTER = NB // SIDE
 
@@ -82,24 +82,26 @@
         cols = chunk_cols(n)
         return pltpu.make_async_copy(m_hbm.at[:, cols], mat.at[:, cols], mat_sem.at[n])
 
-    for n in range(NCH):
+    for n in PAIRS[0]:
         mat_load(n).start()
+
+    barrier = pltpu.get_barrier_semaphore()
+
+    def greet(peer):
+        pl.semaphore_signal(barrier, inc=1, device_id=peer, device_id_type=MESH)
+
+    @pl.when(core == 1)
+    def _():
+        for column in line:
+            greet((prow, column + 1))
+        greet(twin)
+
+    for row, _ in x_peers + y_peers:
+        greet((row, z * 2))
     for copy in loads[2:]:
         copy.start()
-
-    barrier = pltpu.get_barrier_semaphore()
-
-    def greet(peer):
-        pl.semaphore_signal(barrier, inc=1, device_id=peer, device_id_type=MESH)
-
-    for row, _ in x_peers + y_peers:
-        greet((row, z * 2))
-
-    @pl.when(core == 1)
-    def _():
-        greet(twin)
-        for column in line:
-            greet((prow, column + 1))
+    for n in PAIRS[1]:
+        mat_load(n).start()
 
     def remote(src, dst, send_sem, recv_sem, peer):
         return pltpu.make_async_remote_copy(
@@ -200,19 +202,11 @@
             contrib[:, cols] = jnp.where(top, block, picked[0:NB])
             q = (n % 2) * 2 + n // 2
             kept_here[pl.ds(2 * q, 2), :] = picked[NB : NB + 2] + picked[NB + 8 : NB + 10]
-        if pair == PAIRS[0]:
-            @on(1)
-            def _():
-                done(own_rows, rs.at[3])
-
-        for n in pair:
-            begin(up_outer(n))
-
-    @on(1)
-    def _():
-        lbuf[z, 1] = own_rows[...]
-        pl.semaphore_wait(barrier, len(line))
-        begin(z1)
+
+        @on(0)
+        def _():
+            for n in pair:
+                begin(up_outer(n))
 
     holders = piv_cols >> 8
     owners[...] = holders
@@ -220,6 +214,15 @@
     owners_b[1] = holders >> 2
     loads[3].wait()
     linv_high[...], linv_low[...] = split(linv[...])
+
+    @on(1)
+    def _():
+        lbuf[z, 1] = own_rows[...]
+        done(own_rows, rs.at[3])
+        for n in range(NCH):
+            begin(up_outer(n))
+        pl.semaphore_wait(barrier, len(line))
+        begin(z1)
 
     for n in range(NCH):
         r = rings[n % 2]

time: 36.1 us -> 35.9 us (level)
  no operation moved by 1% of the time
where the time goes in v4:
time: 35.9 us; the launch traced here: 35.8 us
  Pallas kernels  35.1 us (98%)
  between operations  0.64 us (2%)
    pallas_call x1, Pallas kernels, shards(): pl.pallas_call(functools.partial(kernel, nz), out_shape=(vmem((NB, column...  34.1 us
    pallas_call x1, Pallas kernels, shards(): pl.pallas_call(hand_over, out_shape=(jax.ShapeDtypeStruct((NB, columns),...  1 us

profile of v4, /device:TPU:1, one launch (start us, length us, event | category | flops | bytes accessed | tf_op | source)
XLA Modules:
  0.0 35.8 jit_solution(13685501333103083940)
XLA Ops:
  0.6 34.1 %shard_map.68 = (f32[256,1024]{1,0:T(8,128)S(1)}, f32[2,1024]{1,0:T(2,128)S(1)}) custom-call(f32[256,1024]{1,0:T(8,128)} %m_hbm.1, f32[8,256]{1,0:T(8,128)} %l_hbm.1, f32[256,256]{1,0:T(8,128)} %linv_hbm.1, s32[1,256]{1,0:T(1,128)} %bitcast.1, f32[2,256]{1,0:T(2,128)} %w_hbm.1), custom_call_target="tpu_custom_call" | custom-call | flops 500000000 | bytes 4000000 | tf_op jit(solution)/shard_map/pallas_call | solution.py:356
  34.8 1.0 %shard_map.69 = (f32[256,1024]{1,0:T(8,128)}, f32[2,1024]{1,0:T(2,128)}) custom-call(f32[256,1024]{1,0:T(8,128)S(1)} %get-tuple-element.4.updated, f32[2,1024]{1,0:T(2,128)S(1)} %get-tuple-element.5.checks), custom_call_target="tpu_custom_call" | custom-call | bytes 2000000 | tf_op jit(solution)/shard_map/pallas_call | solution.py:400

commit v5 on v4

--- a/solution.py
+++ b/solution.py
@@ -34,7 +34,7 @@
 
 def few_rows(rows, wide):
     pair = jnp.concatenate([piece.astype(jnp.float32) for piece in split(rows)], axis=0).astype(jnp.bfloat16)
-    product = sum(bdot(pair, piece) for piece in reversed(wide))
+    product = bdot(jnp.concatenate([pair] * len(wide), axis=1), jnp.concatenate(wide[::-1], axis=0))
     return product[0:8] + product[8:16]
 
 
@@ -48,7 +48,7 @@
     out_ref, chk_ref,
     mat, contrib, owners, owners_b, linv, piv, w8, own_rows, lbuf, vbuf,
     up1, t1s, v1s, up2, esend, slots,
-    linv_high, linv_low, picks, places, factor_high, factor_low, rows_high, rows_low, given, gathered, sums, totals,
+    linv3, picks, factors, rows_high, rows_low, given, gathered, sums, totals,
     load_sem, mat_sem,
     ru, r2, rd, ss, rs,
 ):
@@ -126,10 +126,10 @@
     lane_ids = lax.broadcasted_iota(jnp.int32, (NB, NB), 1)
     piv_cols = jnp.transpose(jnp.broadcast_to(piv[...], (NB, NB)))
     pick = jnp.where(piv_cols - base == lane_ids, 1.0, 0.0)
-    picks[pl.ds(0, NB), :] = pick.astype(jnp.bfloat16)
+    picks[pl.ds(0, NB), :] = jnp.concatenate([pick.astype(jnp.bfloat16)] * 2, axis=1)
     keep_row = 1.0 - jnp.sum(pick, axis=0, keepdims=True)
     kept = jnp.concatenate([piece.astype(jnp.float32) for piece in split(w8[...] * keep_row)], axis=0)
-    picks[pl.ds(NB, 16), :] = kept.astype(jnp.bfloat16)
+    picks[pl.ds(NB, 16), :] = jnp.concatenate([kept.astype(jnp.bfloat16)] * 2, axis=1)
 
     def ring_of(half):
         a, b = (x, y) if half == 0 else (y, x)
@@ -198,7 +198,7 @@
             cols = chunk_cols(n)
             block = mat[:, cols]
             high, middle = split(block)
-            picked = bdot(picks[...], middle) + bdot(picks[...], high)
+            picked = bdot(picks[...], jnp.concatenate([middle, high], axis=0))
             contrib[:, cols] = jnp.where(top, block, picked[0:NB])
             q = (n % 2) * 2 + n // 2
             kept_here[pl.ds(2 * q, 2), :] = picked[NB : NB + 2] + picked[NB + 8 : NB + 10]
@@ -213,7 +213,9 @@
     owners_b[0] = holders & (SIDE - 1)
     owners_b[1] = holders >> 2
     loads[3].wait()
-    linv_high[...], linv_low[...] = split(linv[...])
+    linv_high, linv_low = split(linv[...])
+    linv3[...] = jnp.concatenate([linv_high, linv_low, linv_high], axis=0)
+    factors[:, pl.ds(3 * NB, 2 * NB)] = jnp.concatenate([place.astype(jnp.bfloat16)] * 2, axis=1)
 
     @on(1)
     def _():
@@ -283,11 +285,9 @@
 
     checked[...] = few_rows(w8[...], (lower_high, lower_low))[0:2]
     begin(c5)
-    multiplier = -(
-        (bdot(lower_low, linv_high[...]) + bdot(lower_high, linv_low[...])) + bdot(lower_high, linv_high[...])
-    )
-    factor_high[...], factor_low[...] = split(multiplier)
-    places[...] = place.astype(jnp.bfloat16)
+    multiplier = -bdot(jnp.concatenate([lower_low, lower_high, lower_high], axis=1), linv3[...])
+    high, low_part = split(multiplier)
+    factors[:, pl.ds(0, 3 * NB)] = jnp.concatenate([low_part, high, high], axis=1)
 
     for pair in PAIRS:
         for n in pair:
@@ -299,13 +299,12 @@
             high, low_part = split(jnp.where(owners[...] == prow, contrib[:, cols], got))
             rows_high[:, cols] = high
             rows_low[:, cols] = low_part
-            product = (bdot(factor_low[...], high) + bdot(factor_high[...], low_part)) + bdot(factor_high[...], high)
-            landing = bdot(places[...], got_low) + bdot(places[...], got_high)
-            out_ref[:, cols] = (mat[:, cols] * keep_col + landing) + product
+            product = bdot(factors[...], jnp.concatenate([high, low_part, high, got_low, got_high], axis=0))
+            out_ref[:, cols] = mat[:, cols] * keep_col + product
 
     done(vbuf.at[1:], rs.at[8])
     u = jnp.concatenate([jnp.sum(vbuf[...], axis=0), jnp.zeros((6, NB), jnp.float32)], axis=0)
-    check_factor = -few_rows(u, (linv_high[...], linv_low[...]))
+    check_factor = -few_rows(u, (linv3[pl.ds(0, NB), :], linv3[pl.ds(NB, NB), :]))
 
     done(sums.at[1:], rs.at[7])
     totals[...] = jnp.sum(sums[...], axis=0)
@@ -375,12 +374,9 @@
             vmem((n, 3, QUARTER, W), f32),
             vmem((n, 3, QUARTER, W), f32),
             vmem((NB, columns), f32),
-            vmem((NB, NB), jnp.bfloat16),
-            vmem((NB, NB), jnp.bfloat16),
-            vmem((NB + 16, NB), jnp.bfloat16),
-            vmem((NB, NB), jnp.bfloat16),
-            vmem((NB, NB), jnp.bfloat16),
-            vmem((NB, NB), jnp.bfloat16),
+            vmem((3 * NB, NB), jnp.bfloat16),
+            vmem((NB + 16, 2 * NB), jnp.bfloat16),
+            vmem((NB, 5 * NB), jnp.bfloat16),
             vmem((NB, columns), jnp.bfloat16),
             vmem((NB, columns), jnp.bfloat16),
             vmem((8, NB), f32),

time: 35.9 us -> 35.9 us (level)
  no operation moved by 1% of the time
where the time goes in v5:
time: 35.9 us; the launch traced here: 35.8 us
  Pallas kernels  35.1 us (98%)
  between operations  0.64 us (2%)
    pallas_call x1, Pallas kernels, shards(): pl.pallas_call(functools.partial(kernel, nz), out_shape=(vmem((NB, column...  34.1 us
    pallas_call x1, Pallas kernels, shards(): pl.pallas_call(hand_over, out_shape=(jax.ShapeDtypeStruct((NB, columns),...  1 us

profile of v5, /device:TPU:1, one launch (start us, length us, event | category | flops | bytes accessed | tf_op | source)
XLA Modules:
  0.0 35.8 jit_solution(2747861217585453465)
XLA Ops:
  0.6 34.1 %shard_map.68 = (f32[256,1024]{1,0:T(8,128)S(1)}, f32[2,1024]{1,0:T(2,128)S(1)}) custom-call(f32[256,1024]{1,0:T(8,128)} %m_hbm.1, f32[8,256]{1,0:T(8,128)} %l_hbm.1, f32[256,256]{1,0:T(8,128)} %linv_hbm.1, s32[1,256]{1,0:T(1,128)} %bitcast.1, f32[2,256]{1,0:T(2,128)} %w_hbm.1), custom_call_target="tpu_custom_call" | custom-call | flops 500000000 | bytes 4000000 | tf_op jit(solution)/shard_map/pallas_call | solution.py:355
  34.8 1.0 %shard_map.69 = (f32[256,1024]{1,0:T(8,128)}, f32[2,1024]{1,0:T(2,128)}) custom-call(f32[256,1024]{1,0:T(8,128)S(1)} %get-tuple-element.4.updated, f32[2,1024]{1,0:T(2,128)S(1)} %get-tuple-element.5.checks), custom_call_target="tpu_custom_call" | custom-call | bytes 2000000 | tf_op jit(solution)/shard_map/pallas_call | solution.py:396

commit v6 on v5

--- a/solution.py
+++ b/solution.py
@@ -223,8 +223,13 @@
         done(own_rows, rs.at[3])
         for n in range(NCH):
             begin(up_outer(n))
+
+    def gather_panel():
         pl.semaphore_wait(barrier, len(line))
         begin(z1)
+
+    ahead = z < nz // 8
+    pl.when(jnp.logical_and(core == 1, jnp.logical_not(ahead)))(gather_panel)
 
     for n in range(NCH):
         r = rings[n % 2]
@@ -262,6 +267,8 @@
             esend[n, d - 1] = jnp.where(who == r.who[d], t3, p3)
         slots[rows, chunk_cols(n)] = jnp.where(who == prow, t3, p3)
         begin(down_outer(n))
+
+    pl.when(jnp.logical_and(core == 1, ahead))(gather_panel)
 
     @pl.when(top)
     def _():

time: 35.9 us -> 35.6 us (level)
  no operation moved by 1% of the time
where the time goes in v6:
time: 35.6 us; the launch traced here: 35.4 us
  Pallas kernels  34.8 us (98%)
  between operations  0.64 us (2%)
    pallas_call x1, Pallas kernels, shards(): pl.pallas_call(functools.partial(kernel, nz), out_shape=(vmem((NB, column...  33.8 us
    pallas_call x1, Pallas kernels, shards(): pl.pallas_call(hand_over, out_shape=(jax.ShapeDtypeStruct((NB, columns),...  1 us

profile of v6, /device:TPU:1, one launch (start us, length us, event | category | flops | bytes accessed | tf_op | source)
XLA Modules:
  0.0 35.4 jit_solution(10216511190876075917)
XLA Ops:
  0.6 33.8 %shard_map.68 = (f32[256,1024]{1,0:T(8,128)S(1)}, f32[2,1024]{1,0:T(2,128)S(1)}) custom-call(f32[256,1024]{1,0:T(8,128)} %m_hbm.1, f32[8,256]{1,0:T(8,128)} %l_hbm.1, f32[256,256]{1,0:T(8,128)} %linv_hbm.1, s32[1,256]{1,0:T(1,128)} %bitcast.1, f32[2,256]{1,0:T(2,128)} %w_hbm.1), custom_call_target="tpu_custom_call" | custom-call | flops 500000000 | bytes 4000000 | tf_op jit(solution)/shard_map/pallas_call | solution.py:362
  34.5 1.0 %shard_map.69 = (f32[256,1024]{1,0:T(8,128)}, f32[2,1024]{1,0:T(2,128)}) custom-call(f32[256,1024]{1,0:T(8,128)S(1)} %get-tuple-element.4.updated, f32[2,1024]{1,0:T(2,128)S(1)} %get-tuple-element.5.checks), custom_call_target="tpu_custom_call" | custom-call | bytes 2000000 | tf_op jit(solution)/shard_map/pallas_call | solution.py:403

commit v7 on v5

--- a/solution.py
+++ b/solution.py
@@ -61,7 +61,7 @@
     y_peers = [(x * SIDE + lax.rem(y + d, SIDE), pcol) for d in (1, 2, 3)]
     far_first = sorted(range(1, nz), key=lambda d: -min(d, nz - d))
     line = [lax.rem(z + d, nz) * 2 for d in far_first]
-    z_peers = [(prow, column + 1) for column in line]
+    z_peers = [(prow, column) for column in line]
     plane_peers = [(lax.rem(prow + d, SIDE * SIDE), pcol) for d in range(1, SIDE * SIDE)]
     twin = (prow, z * 2 + 1 - core)
 
@@ -90,14 +90,14 @@
     def greet(peer):
         pl.semaphore_signal(barrier, inc=1, device_id=peer, device_id_type=MESH)
 
-    @pl.when(core == 1)
+    @pl.when(core == 0)
     def _():
         for column in line:
-            greet((prow, column + 1))
+            greet((prow, column))
         greet(twin)
 
     for row, _ in x_peers + y_peers:
-        greet((row, z * 2))
+        greet((row, z * 2 + 1))
     for copy in loads[2:]:
         copy.start()
     for n in PAIRS[1]:
@@ -174,7 +174,7 @@
         ]
 
     checked, kept_here = vbuf.at[prow], sums.at[prow]
-    rows_over = [remote(own_rows, lbuf.at[z, 0], ss.at[3], rs.at[3], twin)]
+    rows_over = [remote(own_rows, lbuf.at[z, 1], ss.at[3], rs.at[3], twin)]
     z1 = [remote(lbuf.at[z], lbuf.at[z], ss.at[4], rs.at[4], peer) for peer in z_peers]
     z2 = [remote(lbuf, lbuf, ss.at[5], rs.at[5], twin)]
     to_top = [remote(given, gathered.at[prow], ss.at[6], rs.at[6], (0, pcol))]
@@ -183,7 +183,7 @@
 
     loads[2].wait()
 
-    @on(0)
+    @on(1)
     def _():
         pl.semaphore_wait(barrier, 13)
         begin(rows_over)
@@ -203,7 +203,7 @@
             q = (n % 2) * 2 + n // 2
             kept_here[pl.ds(2 * q, 2), :] = picked[NB : NB + 2] + picked[NB + 8 : NB + 10]
 
-        @on(0)
+        @on(1)
         def _():
             for n in pair:
                 begin(up_outer(n))
@@ -217,9 +217,9 @@
     linv3[...] = jnp.concatenate([linv_high, linv_low, linv_high], axis=0)
     factors[:, pl.ds(3 * NB, 2 * NB)] = jnp.concatenate([place.astype(jnp.bfloat16)] * 2, axis=1)
 
-    @on(1)
-    def _():
-        lbuf[z, 1] = own_rows[...]
+    @on(0)
+    def _():
+        lbuf[z, 0] = own_rows[...]
         done(own_rows, rs.at[3])
         for n in range(NCH):
             begin(up_outer(n))
@@ -272,12 +272,12 @@
 
     begin(shared)
 
-    @on(1)
+    @on(0)
     def _():
         done(lbuf.at[1:], rs.at[4])
         begin(z2)
 
-    @on(0)
+    @on(1)
     def _():
         done(lbuf, rs.at[5])
 
@@ -319,11 +319,11 @@
     done(sums.at[1:], ss.at[7])
     done(vbuf.at[1:], ss.at[8])
 
+    @on(1)
+    def _():
+        done(own_rows, ss.at[3])
+
     @on(0)
-    def _():
-        done(own_rows, ss.at[3])
-
-    @on(1)
     def _():
         done(lbuf.at[1:], ss.at[4])
         done(lbuf, ss.at[5])

time: 35.9 us -> 35.4 us (0.986)
  Pallas kernels: 35.1 us -> 34.6 us
    pallas_call x1, Pallas kernels: 34.1 us -> 33.6 us  [shards(): pl.pallas_call(functools.partial(kernel, nz), out_shape=(vmem((NB, column...]
where the time goes in v7:
time: 35.4 us; the launch traced here: 35.2 us
  Pallas kernels  34.6 us (98%)
  between operations  0.64 us (2%)
    pallas_call x1, Pallas kernels, shards(): pl.pallas_call(functools.partial(kernel, nz), out_shape=(vmem((NB, column...  33.6 us
    pallas_call x1, Pallas kernels, shards(): pl.pallas_call(hand_over, out_shape=(jax.ShapeDtypeStruct((NB, columns),...  1 us

profile of v7, /device:TPU:1, one launch (start us, length us, event | category | flops | bytes accessed | tf_op | source)
XLA Modules:
  0.0 35.2 jit_solution(8519117047107759995)
XLA Ops:
  0.6 33.6 %shard_map.68 = (f32[256,1024]{1,0:T(8,128)S(1)}, f32[2,1024]{1,0:T(2,128)S(1)}) custom-call(f32[256,1024]{1,0:T(8,128)} %m_hbm.1, f32[8,256]{1,0:T(8,128)} %l_hbm.1, f32[256,256]{1,0:T(8,128)} %linv_hbm.1, s32[1,256]{1,0:T(1,128)} %bitcast.1, f32[2,256]{1,0:T(2,128)} %w_hbm.1), custom_call_target="tpu_custom_call" | custom-call | flops 500000000 | bytes 4000000 | tf_op jit(solution)/shard_map/pallas_call | solution.py:355
  34.2 1.0 %shard_map.69 = (f32[256,1024]{1,0:T(8,128)}, f32[2,1024]{1,0:T(2,128)}) custom-call(f32[256,1024]{1,0:T(8,128)S(1)} %get-tuple-element.4.updated, f32[2,1024]{1,0:T(2,128)S(1)} %get-tuple-element.5.checks), custom_call_target="tpu_custom_call" | custom-call | bytes 2000000 | tf_op jit(solution)/shard_map/pallas_call | solution.py:396

commit v8 on v7

--- a/solution.py
+++ b/solution.py
@@ -263,6 +263,11 @@
         slots[rows, chunk_cols(n)] = jnp.where(who == prow, t3, p3)
         begin(down_outer(n))
 
+    @on(0)
+    def _():
+        done(lbuf.at[1:], rs.at[4])
+        begin(z2)
+
     @pl.when(top)
     def _():
         done(gathered.at[1:], rs.at[6])
@@ -271,11 +276,6 @@
             kept_here[pl.ds(2 * q, 2), :] = part[0:2, q * W : (q + 1) * W]
 
     begin(shared)
-
-    @on(0)
-    def _():
-        done(lbuf.at[1:], rs.at[4])
-        begin(z2)
 
     @on(1)
     def _():

time: 35.4 us -> 35.2 us (level)
  no operation moved by 1% of the time
where the time goes in v8:
time: 35.2 us; the launch traced here: 35.1 us
  Pallas kernels  34.4 us (98%)
  between operations  0.64 us (2%)
    pallas_call x1, Pallas kernels, shards(): pl.pallas_call(functools.partial(kernel, nz), out_shape=(vmem((NB, column...  33.4 us
    pallas_call x1, Pallas kernels, shards(): pl.pallas_call(hand_over, out_shape=(jax.ShapeDtypeStruct((NB, columns),...  1 us

profile of v8, /device:TPU:1, one launch (start us, length us, event | category | flops | bytes accessed | tf_op | source)
XLA Modules:
  0.0 35.1 jit_solution(15670500197844331576)
XLA Ops:
  0.6 33.4 %shard_map.68 = (f32[256,1024]{1,0:T(8,128)S(1)}, f32[2,1024]{1,0:T(2,128)S(1)}) custom-call(f32[256,1024]{1,0:T(8,128)} %m_hbm.1, f32[8,256]{1,0:T(8,128)} %l_hbm.1, f32[256,256]{1,0:T(8,128)} %linv_hbm.1, s32[1,256]{1,0:T(1,128)} %bitcast.1, f32[2,256]{1,0:T(2,128)} %w_hbm.1), custom_call_target="tpu_custom_call" | custom-call | flops 500000000 | bytes 4000000 | tf_op jit(solution)/shard_map/pallas_call | solution.py:355
  34.1 1.0 %shard_map.69 = (f32[256,1024]{1,0:T(8,128)}, f32[2,1024]{1,0:T(2,128)}) custom-call(f32[256,1024]{1,0:T(8,128)S(1)} %get-tuple-element.4.updated, f32[2,1024]{1,0:T(2,128)S(1)} %get-tuple-element.5.checks), custom_call_target="tpu_custom_call" | custom-call | bytes 2000000 | tf_op jit(solution)/shard_map/pallas_call | solution.py:396

commit v9 on v8

--- a/solution.py
+++ b/solution.py
@@ -65,6 +65,14 @@
     plane_peers = [(lax.rem(prow + d, SIDE * SIDE), pcol) for d in range(1, SIDE * SIDE)]
     twin = (prow, z * 2 + 1 - core)
 
+    barrier = pltpu.get_barrier_semaphore()
+
+    def greet(peer):
+        pl.semaphore_signal(barrier, inc=1, device_id=peer, device_id_type=MESH)
+
+    for row, _ in x_peers + y_peers:
+        greet((row, z * 2 + 1))
+
     w8[...] = jnp.zeros_like(w8)
     loads = [
         pltpu.make_async_copy(piv_hbm, piv, load_sem.at[0]),
@@ -85,19 +93,12 @@
     for n in PAIRS[0]:
         mat_load(n).start()
 
-    barrier = pltpu.get_barrier_semaphore()
-
-    def greet(peer):
-        pl.semaphore_signal(barrier, inc=1, device_id=peer, device_id_type=MESH)
-
     @pl.when(core == 0)
     def _():
+        greet(twin)
         for column in line:
             greet((prow, column))
-        greet(twin)
-
-    for row, _ in x_peers + y_peers:
-        greet((row, z * 2 + 1))
+
     for copy in loads[2:]:
         copy.start()
     for n in PAIRS[1]:

time: 35.2 us -> 35.5 us (level)
  no operation moved by 1% of the time
where the time goes in v9:
time: 35.5 us; the launch traced here: 35.4 us
  Pallas kernels  34.7 us (98%)
  between operations  0.64 us (2%)
    pallas_call x1, Pallas kernels, shards(): pl.pallas_call(functools.partial(kernel, nz), out_shape=(vmem((NB, column...  33.7 us
    pallas_call x1, Pallas kernels, shards(): pl.pallas_call(hand_over, out_shape=(jax.ShapeDtypeStruct((NB, columns),...  1 us

profile of v9, /device:TPU:1, one launch (start us, length us, event | category | flops | bytes accessed | tf_op | source)
XLA Modules:
  0.0 35.4 jit_solution(16669937338479108243)
XLA Ops:
  0.6 33.7 %shard_map.68 = (f32[256,1024]{1,0:T(8,128)S(1)}, f32[2,1024]{1,0:T(2,128)S(1)}) custom-call(f32[256,1024]{1,0:T(8,128)} %m_hbm.1, f32[8,256]{1,0:T(8,128)} %l_hbm.1, f32[256,256]{1,0:T(8,128)} %linv_hbm.1, s32[1,256]{1,0:T(1,128)} %bitcast.1, f32[2,256]{1,0:T(2,128)} %w_hbm.1), custom_call_target="tpu_custom_call" | custom-call | flops 500000000 | bytes 4000000 | tf_op jit(solution)/shard_map/pallas_call | solution.py:356
  34.4 1.0 %shard_map.69 = (f32[256,1024]{1,0:T(8,128)}, f32[2,1024]{1,0:T(2,128)}) custom-call(f32[256,1024]{1,0:T(8,128)S(1)} %get-tuple-element.4.updated, f32[2,1024]{1,0:T(2,128)S(1)} %get-tuple-element.5.checks), custom_call_target="tpu_custom_call" | custom-call | bytes 2000000 | tf_op jit(solution)/shard_map/pallas_call | solution.py:397

commit v10 on v8

--- a/solution.py
+++ b/solution.py
@@ -188,10 +188,8 @@
         pl.semaphore_wait(barrier, 13)
         begin(rows_over)
 
-    place = jnp.where(piv[...] - base == row_ids, 1.0, 0.0)
-
-
-    for pair in PAIRS:
+
+    for pair in ((0,), (1,), (2,), (3,)):
         for n in pair:
             mat_load(n).wait()
         for n in pair:
@@ -208,6 +206,7 @@
             for n in pair:
                 begin(up_outer(n))
 
+    place = jnp.where(piv[...] - base == row_ids, 1.0, 0.0)
     holders = piv_cols >> 8
     owners[...] = holders
     owners_b[0] = holders & (SIDE - 1)

time: 35.2 us -> 35.6 us (1.011)
  Pallas kernels: 34.4 us -> 34.8 us
where the time goes in v10:
time: 35.6 us; the launch traced here: 35.4 us
  Pallas kernels  34.8 us (98%)
  between operations  0.64 us (2%)
    pallas_call x1, Pallas kernels, shards(): pl.pallas_call(functools.partial(kernel, nz), out_shape=(vmem((NB, column...  33.8 us
    pallas_call x1, Pallas kernels, shards(): pl.pallas_call(hand_over, out_shape=(jax.ShapeDtypeStruct((NB, columns),...  1 us

profile of v10, /device:TPU:1, one launch (start us, length us, event | category | flops | bytes accessed | tf_op | source)
XLA Modules:
  0.0 35.4 jit_solution(11345587513913046626)
XLA Ops:
  0.6 33.8 %shard_map.68 = (f32[256,1024]{1,0:T(8,128)S(1)}, f32[2,1024]{1,0:T(2,128)S(1)}) custom-call(f32[256,1024]{1,0:T(8,128)} %m_hbm.1, f32[8,256]{1,0:T(8,128)} %l_hbm.1, f32[256,256]{1,0:T(8,128)} %linv_hbm.1, s32[1,256]{1,0:T(1,128)} %bitcast.1, f32[2,256]{1,0:T(2,128)} %w_hbm.1), custom_call_target="tpu_custom_call" | custom-call | flops 500000000 | bytes 4000000 | tf_op jit(solution)/shard_map/pallas_call | solution.py:354
  34.4 1.0 %shard_map.69 = (f32[256,1024]{1,0:T(8,128)}, f32[2,1024]{1,0:T(2,128)}) custom-call(f32[256,1024]{1,0:T(8,128)S(1)} %get-tuple-element.4.updated, f32[2,1024]{1,0:T(2,128)S(1)} %get-tuple-element.5.checks), custom_call_target="tpu_custom_call" | custom-call | bytes 2000000 | tf_op jit(solution)/shard_map/pallas_call | solution.py:395
